TPU v7x, 256 devices: a whole 4x4x8 slice. The times are simulated.
256 devices in a mesh: occ: 16 (over y, z_lo), aux: 16 (over z_hi, x, core).
Axes of the slice: x: 4, y: 4, z: 8 (z_hi: 2, z_lo: 4; z = z_hi * 4 + z_lo), core: 2. Of those that a mesh axis runs over, the one named last changes fastest.
Arguments:
- three_index: bfloat16 [6144, 32, 1536], P(('occ', 'aux')), may hold values from -0.099609375 to 0.099609375
- occupied_energy: float32 [32], replicated, may hold values from -1.5 to -0.3
- virtual_energy: float32 [1536], replicated, may hold values from 0.2 to 4
- pair_list: int32 [16, 2], P('occ'), may hold values from 0 to 31, as said below
Outputs:
- density: float32 [1536, 1536], P('aux', 'occ')
Inputs may be any that keep to these rules, and one draw needn't show every extreme that they name: `pair_list`: row o + r is the pair handled by occupied block o in round r: its first index lies in o * 2 to o * 2 + 1, and in each round r the second indices of all 16 rows of that round lie in one common block of 2 consecutive orbitals starting at a multiple of 2.
All inputs are finite; a program needn't handle non-finite values.
Results may differ from a plain program's by a relative error of at most 0.0003.
Values may be sent and summed in bfloat16 or wider, within the bound.
A program may use at most 64 MiB of HBM per device.

v0:
```python
import jax
import jax.numpy as jnp
from jax import lax
from jax.sharding import PartitionSpec as P


def broadcast(block, axis, owner):
    block = jnp.where(lax.axis_index(axis) == owner, block, jnp.zeros_like(block))
    return lax.psum(block, axis)


def shards(three_index, occupied_energy, virtual_energy, pair_list):
    blocks = lax.all_to_all(three_index, "occ", split_axis=1, concat_axis=0, tiled=True)
    block_width = blocks.shape[1]
    virtual_count = blocks.shape[2]
    column_share = virtual_count // lax.axis_size("aux")
    aux_position = lax.axis_index("aux")
    own_energy = lax.dynamic_slice_in_dim(virtual_energy, aux_position * column_share, column_share)
    first_index = pair_list[0, 0]
    second_index = pair_list[0, 1]
    owner_slab = broadcast(blocks, "occ", second_index // block_width)
    left_slab = lax.dynamic_index_in_dim(blocks, first_index % block_width, 1, keepdims=False)
    right_slab = lax.dynamic_index_in_dim(owner_slab, second_index % block_width, 1, keepdims=False)
    shift_energy = occupied_energy[first_index] + occupied_energy[second_index]
    denominator = own_energy[:, None] + virtual_energy[None, :] - shift_energy
    flipped = lax.psum_scatter(
        lax.dot_general(
            right_slab, left_slab, (((0,), (0,)), ((), ())), preferred_element_type=jnp.float32
        ),
        "aux",
        scatter_dimension=0,
        tiled=True,
    )
    amplitudes = -flipped / denominator
    accumulated = lax.dot_general(
        amplitudes,
        amplitudes,
        (((0,), (0,)), ((), ())),
        precision=lax.Precision.HIGHEST,
        preferred_element_type=jnp.float32,
    )
    reduced = lax.psum_scatter(accumulated, "occ", scatter_dimension=1, tiled=True)
    density = lax.psum_scatter(reduced, "aux", scatter_dimension=0, tiled=True)
    return density


def solution(mesh):
    placed = (P(("occ", "aux"), None, None), P(), P(), P("occ", None))
    return jax.shard_map(
        shards, mesh=mesh, in_specs=placed, out_specs=P("aux", "occ"), check_vma=False
    )
```

profile of v0, /device:TPU:8, one launch (start us, length us, event | category | flops | bytes accessed | tf_op | source)
XLA Modules:
  0.0 716.3 jit_solution(6860869556890927656)
XLA Ops:
  6.5 4.4 copy.10
  10.9 0.0 copy-start.3
  10.9 9.1 %all-to-all-start = ((bf16[24,32,1536]{2,0,1:T(8,128)(2,1)}), bf16[24,32,1536]{2,0,1:T(8,128)(2,1)S(1)}, u32[]{:S(2)}, u32[]{:S(2)}) async-start(bf16[24,32,1536]{2,0,1:T(8,128)(2,1)} %copy.10), calls=%async_computation | async-start | bytes 4718592 | tf_op jit(solution)/shard_map/all_to_all | solution.py:13
  20.0 0.0 all-reduce.2.cloned.1.call-start
  20.1 0.0 copy-done.3
  20.1 0.6 fusion.15
  23.3 50.5 %all-to-all-done = bf16[24,32,1536]{2,0,1:T(8,128)(2,1)S(1)} async-done(((bf16[24,32,1536]{2,0,1:T(8,128)(2,1)}), bf16[24,32,1536]{2,0,1:T(8,128)(2,1)S(1)}, u32[]{:S(2)}, u32[]{:S(2)}) %all-to-all-start) | async-done | bytes 2359328 | tf_op jit(solution)/shard_map/all_to_all | solution.py:13
  73.8 0.0 copy-start
  73.8 1.4 copy-done
  75.2 1.8 copy.11
  77.0 1.7 broadcast_select_fusion
  78.8 0.0 all-reduce.2.cloned.1.call-update
  78.8 0.0 reduce-scatter.6.cloned.1.call-start
  80.7 170.8 %all-reduce.2.cloned.1.call-done = bf16[384,2,1536]{2,0,1:T(8,128)(2,1)} async-done(((bf16[384,2,1536]{2,0,1:T(8,128)(2,1)}), bf16[384,2,1536]{2,0,1:T(8,128)(2,1)}) %all-reduce.2.cloned.1.call-update) | async-done | bytes 2359312 | tf_op jit(solution)/shard_map/psum | solution.py:9
  251.5 6.4 fusion
  257.9 0.0 copy-start.1
  257.9 0.0 copy-start.2
  257.9 0.0 reduce-scatter.6.cloned.1.call-update
  258.0 0.0 reduce-scatter.8.cloned.1.call-start
  260.6 0.0 copy-done.1
  260.6 0.1 dynamic_slice.18
  260.6 0.0 copy-done.2
  260.6 0.6 fusion.14
  262.6 150.1 %reduce-scatter.6.cloned.1.call-done = f32[96,1536]{1,0:T(8,128)} async-done(((f32[1536,1536]{1,0:T(8,128)}), f32[96,1536]{1,0:T(8,128)}) %reduce-scatter.6.cloned.1.call-update) | async-done | bytes 589840 | tf_op jit(solution)/shard_map/reduce_scatter | solution.py:26
  412.7 11.5 %fusion.5 = f32[1536,1536]{0,1:T(8,128)} fusion(f32[96,1536]{1,0:T(8,128)} %reduce-scatter.6.cloned.1.call-done, f32[]{:T(128)} %bitcast.7, f32[1536]{0:T(1024)S(1)} %copy-done.1, f32[96]{0:T(128)S(1)} %dynamic_slice.18), kind=kOutput, calls=%fused_computation.6 | convolution fusion | flops 2718498816 | bytes 10033540 | tf_op jit(solution)/shard_map/dot_general | solution.py:35
  424.2 0.0 reduce-scatter.8.cloned.1.call-update
  424.2 0.0 reduce-scatter.10.cloned.1.call-start
  424.2 202.9 %reduce-scatter.8.cloned.1.call-done = f32[1536,96]{0,1:T(8,128)} async-done(((f32[1536,1536]{0,1:T(8,128)}), f32[1536,96]{0,1:T(8,128)}) %reduce-scatter.8.cloned.1.call-update) | async-done | bytes 589840 | tf_op jit(solution)/shard_map/reduce_scatter | solution.py:42
  627.2 2.2 copy.13
  629.4 0.0 reduce-scatter.10.cloned.1.call-update
  629.4 80.3 %reduce-scatter.10.cloned.1.call-done = f32[96,96]{1,0:T(8,128)} async-done(((f32[1536,96]{1,0:T(8,128)}), f32[96,96]{1,0:T(8,128)}) %reduce-scatter.10.cloned.1.call-update) | async-done | bytes 36880 | tf_op jit(solution)/shard_map/reduce_scatter | solution.py:43
Async XLA Ops:
  10.9 9.2 %copy-start.3 = (s32[1,2]{1,0:T(1,128)S(1)}, s32[1,2]{1,0:T(1,128)}, u32[]{:S(2)}) copy-start(s32[1,2]{1,0:T(1,128)} %param.7) | copy-start | bytes 28
  10.9 62.9 %all-to-all-start = ((bf16[24,32,1536]{2,0,1:T(8,128)(2,1)}), bf16[24,32,1536]{2,0,1:T(8,128)(2,1)S(1)}, u32[]{:S(2)}, u32[]{:S(2)}) async-start(bf16[24,32,1536]{2,0,1:T(8,128)(2,1)} %copy.10), calls=%async_computation | async-start | bytes 4718592 | tf_op jit(solution)/shard_map/all_to_all | solution.py:13
  20.0 231.5 %all-reduce.2.cloned.1.call-start = ((), (), s32[]{:S(2)}) async-start(), calls=%async_computation.4 | async-start | bytes 4718592 | tf_op jit(solution)/shard_map/psum | solution.py:9
  73.8 1.4 copy-start
  78.8 333.9 %reduce-scatter.6.cloned.1.call-start = ((), (), s32[]{:S(2)}) async-start(), calls=%async_computation.5 | async-start | bytes 10027008 | tf_op jit(solution)/shard_map/reduce_scatter | solution.py:26
  257.9 2.6 copy-start.1
  257.9 2.7 copy-start.2
  258.0 369.2 %reduce-scatter.8.cloned.1.call-start = ((), (), s32[]{:S(2)}) async-start(), calls=%async_computation.6 | async-start | bytes 10027008 | tf_op jit(solution)/shard_map/reduce_scatter | solution.py:42
  424.2 285.6 %reduce-scatter.10.cloned.1.call-start = ((), (), s32[]{:S(2)}) async-start(), calls=%async_computation.7 | async-start | bytes 835584 | tf_op jit(solution)/shard_map/reduce_scatter | solution.py:43
Sparse Core Ops, SparseCore 0:
  78.9 172.5 all-reduce.1
  258.1 154.5 reduce-scatter.5
  424.3 202.8 reduce-scatter.7
  631.1 78.6 reduce-scatter.9
where the time goes:
time: 717 us; the launch traced here: 716 us
  waiting for transfers between devices  655 us (91%)
  between operations  21.5 us (3%)
  matrix products  17.9 us (2%)
  local copies, waits for them, and re-layouts  11.2 us (2%)
  starting transfers between devices  9.29 us (1%)
    reduce_scatter x1, waiting for transfers between devices, shards(): lax.psum_scatter(accumulated, 'occ', scatter_dimension=1, tiled=True)  203 us
    psum x1, waiting for transfers between devices, broadcast(): return lax.psum(block, axis)  171 us
    reduce_scatter x1, waiting for transfers between devices, shards(): lax.psum_scatter(lax.dot_general(right_slab, left_slab, (((0,), (0,)), ((...  150 us
    reduce_scatter x1, waiting for transfers between devices, shards(): density = lax.psum_scatter(reduced, 'aux', scatter_dimension=0, tiled=True)  80.3 us
    all_to_all x1, waiting for transfers between devices, shards(): lax.all_to_all(three_index, 'occ', split_axis=1, concat_axis=0, tiled=True)  50.5 us
  transfers between devices with their start and end apart: 5, of which 5 were waited for; matrix products, arithmetic and copies ran while one was open for 0% of the time, Pallas kernels for 0%

commit v1 on v0

v1 whole, which is shorter than its diff:
```python
import functools

import jax
import jax.numpy as jnp
from jax import lax
from jax.experimental import pallas as pl
from jax.experimental.pallas import tpu as pltpu
from jax.sharding import PartitionSpec as P

MESH = pl.DeviceIdType.MESH
F32 = jnp.float32
BF16 = jnp.bfloat16
I16 = jnp.int16
NX, NY, NZ = 4, 4, 8
PLANE = NX * NY
CODE = 16


def position():
    occ, aux = lax.axis_index("occ"), lax.axis_index("aux")
    core = lax.rem(aux, 2)
    x = lax.rem(lax.div(aux, 2), NX)
    z = lax.div(aux, 2 * NX) * 4 + lax.rem(occ, 4)
    return x, lax.div(occ, 4), z, core


def device(x, y, z, core):
    return (y * 4 + lax.rem(z, 4), (lax.div(z, 4) * NX + x) * 2 + core)


def greet(peers_of, count, others):
    barrier = pltpu.get_barrier_semaphore()

    def signal(k, carry):
        pl.semaphore_signal(barrier, inc=1, device_id=peers_of(k), device_id_type=MESH)
        return carry

    lax.fori_loop(1, count, signal, 0)
    for other in others:
        pl.semaphore_signal(barrier, inc=1, device_id=other, device_id_type=MESH)
    pl.semaphore_wait(barrier, count - 1 + len(others))


def remote(src, dst, send, recv, dev):
    return pltpu.make_async_remote_copy(
        src_ref=src, dst_ref=dst, send_sem=send, recv_sem=recv, device_id=dev, device_id_type=MESH
    )


def exchange_kernel(half, three, pairs, sibling_rows, listed, mine, table, send, recv, half_send, half_recv):
    occ, aux = lax.axis_index("occ"), lax.axis_index("aux")
    x, y, z, core = position()
    sibling = device(x, y, z, 1 - core)

    def peer(k):
        return (lax.rem(occ + k, 16), aux)

    mine[...] = jnp.zeros_like(mine)
    mine[0:1, 0:2] = pairs[...]
    greet(peer, 16, [sibling])
    columns = pl.ds(pl.multiple_of((1 - core) * half, 128), half)
    rows = remote(three.at[:, :, columns], sibling_rows, half_send, half_recv, sibling)

    def copy(k):
        return remote(mine, table.at[occ], send.at[k], recv.at[k], peer(k))

    def start(k, carry):
        copy(k).start()
        return carry

    lax.fori_loop(1, 16, start, 0)
    rows.start()
    table[occ] = mine[...]

    def finish(k, carry):
        copy(k).wait_send()
        came = lax.rem(occ + 16 - k, 16)
        remote(mine, table.at[came], send.at[k], recv.at[k], peer(k)).wait_recv()
        return carry

    lax.fori_loop(1, 16, finish, 0)
    listed[...] = table[...]
    rows.wait()


def exchange(three, pairs, half):
    depth, orbitals, _ = three.shape
    return pl.pallas_call(
        functools.partial(exchange_kernel, half),
        out_shape=(
            jax.ShapeDtypeStruct((depth, orbitals, half), BF16),
            jax.ShapeDtypeStruct((16, 8, 128), jnp.int32),
        ),
        in_specs=[pl.BlockSpec(memory_space=pl.ANY), pl.BlockSpec(memory_space=pltpu.VMEM)],
        out_specs=(pl.BlockSpec(memory_space=pl.ANY), pl.BlockSpec(memory_space=pltpu.VMEM)),
        scratch_shapes=[
            pltpu.VMEM((8, 128), jnp.int32),
            pltpu.VMEM((16, 8, 128), jnp.int32),
            pltpu.SemaphoreType.DMA((16,)),
            pltpu.SemaphoreType.DMA((16,)),
            pltpu.SemaphoreType.DMA,
            pltpu.SemaphoreType.DMA,
        ],
        compiler_params=pltpu.CompilerParams(collective_id=0, has_side_effects=True),
        name="exchange",
    )(three, pairs)


def encode(block, ref):
    rows = block.shape[0]
    top = jnp.maximum(jnp.max(jnp.abs(block), axis=0, keepdims=True), 1e-30)
    level = jnp.ceil(jnp.log(top) * 64.0)
    ref[0:rows, :] = jnp.round(block * (32000.0 * jnp.exp(level * (-1.0 / 64.0)))).astype(jnp.int32).astype(I16)
    ref[rows : rows + CODE, :] = jnp.broadcast_to(level, (CODE, block.shape[1])).astype(jnp.int32).astype(I16)


def decode(ref):
    rows = ref.shape[0] - CODE
    level = ref[rows : rows + CODE, :].astype(jnp.int32).astype(F32)[0:1, :]
    return ref[0:rows, :].astype(jnp.int32).astype(F32) * (jnp.exp(level * (1.0 / 64.0)) * (1.0 / 32000.0))


def dot_rows(a, b):
    return lax.dot_general(a, b, (((0,), (0,)), ((), ())), preferred_element_type=F32)


def density_kernel(
    half, slab, a_msg, b_msg, eb, ea, out,
    a_in, b_in, b_sib, coulomb, up_out, up_in, down_out, down_in, amp, high, low, left_high, left_low,
    dens, y_up0, y_up1, y_down0, y_down1, part, z_up, z_down,
    own_sem, a_send, a_recv, b_send, b_recv, s_send, s_recv, ring_send, ring_recv, x_send, x_recv, c_send, c_recv,
    y_send, y_recv, z_send, z_recv,
):
    x, y, z, core = position()
    me = x * NY + y
    cut = half // 2
    side = out.shape[0]

    def peer(k):
        to = lax.rem(me + k, PLANE)
        return device(lax.div(to, NY), lax.rem(to, NY), z, core)

    sibling = device(x, y, z, 1 - core)
    z_next, z_prev = lax.rem(z + 1, NZ), lax.rem(z + NZ - 1, NZ)
    above, below = device(x, y, z_next, core), device(x, y, z_prev, core)
    greet(peer, PLANE, [sibling, above, below])

    def to_plane(msg, into, send, recv, k):
        return remote(msg.at[lax.rem(me + k, PLANE)], into.at[me], send.at[k], recv.at[k], peer(k))

    def from_plane(msg, into, send, recv, k):
        came = lax.rem(me + PLANE - k, PLANE)
        return remote(msg.at[came], into.at[came], send.at[k], recv.at[k], peer(k))

    def to_sibling(k):
        came = lax.rem(me + PLANE - k, PLANE)
        return remote(b_in.at[came], b_sib.at[came], s_send.at[k], s_recv.at[k], sibling)

    def start_b(k, carry):
        to_plane(b_msg, b_in, b_send, b_recv, k).start()
        return carry

    def start_a(k, carry):
        to_plane(a_msg, a_in, a_send, a_recv, k).start()
        return carry

    lax.fori_loop(1, PLANE, start_b, 0)
    own_b = pltpu.make_async_copy(b_msg.at[me], b_in.at[me], own_sem.at[0])
    own_a = pltpu.make_async_copy(a_msg.at[me], a_in.at[me], own_sem.at[1])
    own_b.start()
    own_a.start()
    lax.fori_loop(1, PLANE, start_a, 0)
    own_b.wait()
    to_sibling(0).start()

    def pass_on(k, carry):
        from_plane(b_msg, b_in, b_send, b_recv, k).wait_recv()
        to_sibling(k).start()
        return carry

    lax.fori_loop(1, PLANE, pass_on, 0)
    own_a.wait()

    def take(k, carry):
        from_plane(a_msg, a_in, a_send, a_recv, k).wait_recv()
        return carry

    lax.fori_loop(1, PLANE, take, 0)

    def take_sibling(k, carry):
        to_sibling(k).wait_recv()
        return carry

    lax.fori_loop(0, PLANE, take_sibling, 0)

    rows_a = a_in[...].reshape(-1, half)
    tile = 256
    for source, which in ((b_in, core), (b_sib, 1 - core)):
        for n in range(half // tile):
            lhs = source[:, :, n * tile : (n + 1) * tile].reshape(-1, tile)
            coulomb[pl.ds(pl.multiple_of(which * half + n * tile, tile), tile), :] = dot_rows(lhs, rows_a)

    def block(w):
        return coulomb[pl.ds(pl.multiple_of(w * slab, slab), slab), :]

    far = block(lax.rem(z + 4, NZ))
    encode(far[:, :cut], up_out.at[0, :, :cut])
    up = [remote(up_out.at[0, :, :cut], up_in.at[0, :, :cut], ring_send.at[0], ring_recv.at[0], above)]
    up[0].start()
    encode(far[:, cut:], down_out.at[0, :, cut:])
    down = [remote(down_out.at[0, :, cut:], down_in.at[0, :, cut:], ring_send.at[4], ring_recv.at[4], below)]
    down[0].start()
    for t in range(1, 4):
        for way, sent, box, into, w, to in (
            (0, up, up_out, up_in, lax.rem(z + 4 - t, NZ), above),
            (1, down, down_out, down_in, lax.rem(z + 4 + t, NZ), below),
        ):
            sent[t - 1].wait_recv()
            mine = block(w)
            if t == 1:
                columns = slice(cut, half) if way else slice(0, cut)
                rest = slice(0, cut) if way else slice(cut, half)
                encode(mine[:, columns] + decode(into.at[0, :, columns]), box.at[t, :, columns])
                encode(mine[:, rest], box.at[t, :, rest])
            else:
                encode(mine + decode(into.at[t - 1]), box.at[t])
            sent.append(remote(box.at[t], into.at[t], ring_send.at[4 * way + t], ring_recv.at[4 * way + t], to))
            sent[t].start()
    own = block(z)
    up[3].wait_recv()
    down[3].wait_recv()
    own = own + decode(up_in.at[3]) + decode(down_in.at[3])

    encode(-own / (eb[...] + ea[...]), amp.at[core, x])
    x_next, x_prev, x_far = lax.rem(x + 1, NX), lax.rem(x + NX - 1, NX), lax.rem(x + 2, NX)
    right, left = device(x_next, y, z, core), device(x_prev, y, z, core)

    def same_slot(k, columns, n, dev):
        ref = amp.at[core, k] if columns is None else amp.at[core, k, :, columns]
        return remote(ref, ref, x_send.at[n], x_recv.at[n], dev)

    def share(k, n):
        return remote(amp.at[core, k], amp.at[core, k], c_send.at[n], c_recv.at[n], sibling)

    def shared(k, n):
        return remote(amp.at[1 - core, k], amp.at[1 - core, k], c_send.at[n], c_recv.at[n], sibling)

    low_cut, high_cut = slice(0, cut), slice(cut, half)
    sends = [same_slot(x, None, 0, right), same_slot(x, None, 1, left), share(x, 0)]
    for s in sends:
        s.start()
    same_slot(x_prev, None, 0, right).wait_recv()
    sends += [same_slot(x_prev, low_cut, 2, right), share(x_prev, 1)]
    for s in sends[-2:]:
        s.start()
    same_slot(x_next, None, 1, left).wait_recv()
    sends += [same_slot(x_next, high_cut, 3, left), share(x_next, 2)]
    for s in sends[-2:]:
        s.start()
    same_slot(x_far, low_cut, 2, right).wait_recv()
    same_slot(x_far, high_cut, 3, left).wait_recv()
    sends.append(share(x_far, 3))
    sends[-1].start()
    for k, n in ((x, 0), (x_prev, 1), (x_next, 2), (x_far, 3)):
        shared(k, n).wait_recv()

    shift = lax.rem(half - side * (x * 2 + core), half)
    for h in range(2):
        for k in range(NX):
            value = decode(amp.at[h, k])
            rows = slice(k * slab, (k + 1) * slab)
            columns = slice(h * half, (h + 1) * half)
            top = value.astype(BF16)
            high[rows, columns] = top
            low[rows, columns] = (value - top.astype(F32)).astype(BF16)
            turned = pltpu.roll(value, shift, 1)[:, 0:128]
            top = turned.astype(BF16)
            left_high[h, rows, :] = top
            left_low[h, rows, :] = (turned - top.astype(F32)).astype(BF16)
    width = dens.shape[3]
    for h in range(2):
        for n in range(NY):
            columns = slice(n * width, (n + 1) * width)
            total = dot_rows(left_high[h], low[:, columns]) + dot_rows(left_low[h], high[:, columns])
            total = total + dot_rows(left_low[h], low[:, columns])
            dens[n, h] = (total + dot_rows(left_high[h], high[:, columns]))[0:side, :]

    y_next, y_prev, y_far = lax.rem(y + 1, NY), lax.rem(y + NY - 1, NY), lax.rem(y + 2, NY)
    north, south = device(x, y_next, z, core), device(x, y_prev, z, core)
    first = remote(dens.at[y_far, 0], y_up0, y_send.at[0], y_recv.at[0], north)
    second = remote(dens.at[y_far, 1], y_down0, y_send.at[1], y_recv.at[1], south)
    first.start()
    second.start()
    first.wait_recv()
    dens[y_next, 0] = dens[y_next, 0] + y_up0[...]
    third = remote(dens.at[y_next], y_up1, y_send.at[2], y_recv.at[2], north)
    third.start()
    second.wait_recv()
    dens[y_prev, 1] = dens[y_prev, 1] + y_down0[...]
    fourth = remote(dens.at[y_prev], y_down1, y_send.at[3], y_recv.at[3], south)
    fourth.start()
    third.wait_recv()
    fourth.wait_recv()
    for h in range(2):
        total = dens[y, h] + y_up1[h] + y_down1[h]
        for n in range(4):
            part[h * 4 + n] = total[:, n * side : (n + 1) * side]

    far_z = lax.rem(z + 4, NZ)
    mid = side // 2
    up_z = [remote(part.at[far_z, :mid], z_up.at[0, :mid], z_send.at[0], z_recv.at[0], above)]
    down_z = [remote(part.at[far_z, mid:], z_down.at[0, mid:], z_send.at[4], z_recv.at[4], below)]
    up_z[0].start()
    down_z[0].start()
    for t in range(1, 4):
        for way, sent, into, w, to in (
            (0, up_z, z_up, lax.rem(z + 4 - t, NZ), above),
            (1, down_z, z_down, lax.rem(z + 4 + t, NZ), below),
        ):
            sent[t - 1].wait_recv()
            if t > 1:
                part[w] = part[w] + into[t - 1]
            elif way:
                part[w, mid:] = part[w, mid:] + into[0, mid:]
            else:
                part[w, :mid] = part[w, :mid] + into[0, :mid]
            sent.append(remote(part.at[w], into.at[t], z_send.at[4 * way + t], z_recv.at[4 * way + t], to))
            sent[t].start()
    up_z[3].wait_recv()
    down_z[3].wait_recv()
    out[...] = part[z] + z_up[3] + z_down[3]

    def drain(k, carry):
        to_plane(b_msg, b_in, b_send, b_recv, k).wait_send()
        to_plane(a_msg, a_in, a_send, a_recv, k).wait_send()
        return carry

    lax.fori_loop(1, PLANE, drain, 0)

    def drain_sibling(k, carry):
        to_sibling(k).wait_send()
        return carry

    lax.fori_loop(0, PLANE, drain_sibling, 0)
    for s in up + down + sends + [first, second, third, fourth] + up_z + down_z:
        s.wait_send()


def density(a_msg, b_msg, eb, ea):
    _, depth, half = a_msg.shape
    virtual = 2 * half
    slab = virtual // NZ
    side = virtual // 16
    coded = slab + CODE
    dma = pltpu.SemaphoreType.DMA
    vmem = pltpu.VMEM
    return pl.pallas_call(
        functools.partial(density_kernel, half, slab),
        out_shape=jax.ShapeDtypeStruct((side, side), F32),
        in_specs=[pl.BlockSpec(memory_space=pl.ANY)] * 2 + [pl.BlockSpec(memory_space=vmem)] * 2,
        out_specs=pl.BlockSpec(memory_space=vmem),
        scratch_shapes=[
            vmem((PLANE, depth, half), BF16),
            vmem((PLANE, depth, half), BF16),
            vmem((PLANE, depth, half), BF16),
            vmem((virtual, half), F32),
            vmem((4, coded, half), I16),
            vmem((4, coded, half), I16),
            vmem((4, coded, half), I16),
            vmem((4, coded, half), I16),
            vmem((2, NX, coded, half), I16),
            vmem((NX * slab, virtual), BF16),
            vmem((NX * slab, virtual), BF16),
            vmem((2, NX * slab, 128), BF16),
            vmem((2, NX * slab, 128), BF16),
            vmem((NY, 2, side, virtual // NY), F32),
            vmem((side, virtual // NY), F32),
            vmem((2, side, virtual // NY), F32),
            vmem((side, virtual // NY), F32),
            vmem((2, side, virtual // NY), F32),
            vmem((NZ, side, side), F32),
            vmem((4, side, side), F32),
            vmem((4, side, side), F32),
            dma((2,)),
            dma((PLANE,)),
            dma((PLANE,)),
            dma((PLANE,)),
            dma((PLANE,)),
            dma((PLANE,)),
            dma((PLANE,)),
            dma((8,)),
            dma((8,)),
            dma((4,)),
            dma((4,)),
            dma((4,)),
            dma((4,)),
            dma((4,)),
            dma((4,)),
            dma((8,)),
            dma((8,)),
        ],
        compiler_params=pltpu.CompilerParams(
            collective_id=1, has_side_effects=True, vmem_limit_bytes=48 * 1024 * 1024
        ),
        name="density",
    )(a_msg, b_msg, eb, ea)


def shards(three_index, occupied_energy, virtual_energy, pair_list):
    depth, orbitals, virtual = three_index.shape
    half = virtual // 2
    slab = virtual // NZ
    x, y, z, core = position()
    sibling_rows, listed = exchange(three_index, pair_list, half)
    pairs = listed[:, 0, 0:2]
    first, second = pairs[:, 0], pairs[:, 1]
    mine = lax.dynamic_slice_in_dim(three_index, core * half, half, axis=2)
    rows = jnp.stack([jnp.where(core == 0, mine, sibling_rows), jnp.where(core == 0, sibling_rows, mine)])
    split = rows.reshape(2, depth, PLANE, 2, half)
    odd = (first % 2 == 1)[None, None, :, None]
    left_rows = jnp.where(odd, split[:, :, :, 1], split[:, :, :, 0])
    a_msg = left_rows.transpose(2, 0, 1, 3).reshape(PLANE, 2 * depth, half)
    common = lax.dynamic_slice_in_dim(rows, pair_list[0, 1] // 2 * 2, 2, axis=2).reshape(2 * depth, 2, half)
    odd = (second % 2 == 1)[:, None, None]
    b_msg = jnp.where(odd, common[None, :, 1], common[None, :, 0])
    own_pair = lax.dynamic_index_in_dim(pairs, x * NY + y, 0, keepdims=False)
    shift_energy = occupied_energy[own_pair[0]] + occupied_energy[own_pair[1]]
    eb = lax.dynamic_slice_in_dim(virtual_energy, z * slab, slab)[:, None]
    ea = lax.dynamic_slice_in_dim(virtual_energy, core * half, half)[None, :] - shift_energy
    return density(a_msg, b_msg, eb, ea)


def solution(mesh):
    placed = (P(("occ", "aux"), None, None), P(), P(), P("occ", None))
    return jax.shard_map(shards, mesh=mesh, in_specs=placed, out_specs=P("aux", "occ"), check_vma=False)
```

time: 717 us -> 152 us (0.21)
  waiting for transfers between devices: 655 us -> 0 us
  Pallas kernels: 0 us -> 128 us
  matrix products: 17.9 us -> 0 us
  between operations: 21.5 us -> 7.84 us
  starting transfers between devices: 9.29 us -> 0 us
    reduce_scatter x3 -> x0, waiting for transfers between devices: 433 us -> none  [the longest x1 203 us: shards(): lax.psum_scatter(accumulated, 'occ', scatter_dimension=1, tiled=True)]
    psum x1 -> x0, waiting for transfers between devices: 171 us -> none  [broadcast(): return lax.psum(block, axis)]
    pallas_call x0 -> x2, Pallas kernels: none -> 128 us  [the longest x1 117 us: density(): pl.pallas_call(functools.partial(density_kernel, half, slab), out_shape=j...]
    all_to_all x1 -> x0, waiting for transfers between devices: 50.5 us -> none  [shards(): lax.all_to_all(three_index, 'occ', split_axis=1, concat_axis=0, tiled=True)]
    dot_general x2 -> x0, matrix products: 17.9 us -> none  [the longest x1 11.5 us: shards(): lax.dot_general(amplitudes, amplitudes, (((0,), (0,)), ((), ())), precisi...]
    all_to_all x1 -> x0, starting transfers between devices: 9.13 us -> none  [shards(): lax.all_to_all(three_index, 'occ', split_axis=1, concat_axis=0, tiled=True)]
  transfers between devices with their start and end apart: 5 -> 0, of which waited for: 5 -> 0; matrix products, arithmetic and copies ran while one was open for 0% -> 0% of each run, Pallas kernels for 0% -> 0%
where the time goes in v1:
time: 152 us
  Pallas kernels  128 us (84%)
  local copies, waits for them, and re-layouts  10.7 us (7%)
  between operations  7.84 us (5%)
  other arithmetic  5.31 us (3%)
    pallas_call x1, Pallas kernels, density(): pl.pallas_call(functools.partial(density_kernel, half, slab), out_shape=j...  117 us
    pallas_call x1, Pallas kernels, exchange(): pl.pallas_call(functools.partial(exchange_kernel, half), out_shape=(jax.S...  11.2 us
    unnamed x8, local copies, waits for them, and re-layouts  3.61 us
    another operation x3, local copies, waits for them, and re-layouts, shards(): jnp.stack([jnp.where(core == 0, mine, sibling_rows), jnp.where(core == 0,...  3.49 us

profile of v1, /device:TPU:8, one launch (start us, length us, event | category | flops | bytes accessed | tf_op | source)
XLA Modules:
  0.0 151.7 jit_solution(7833680822933124218)
XLA Ops:
  0.0 0.0 copy-start.1
  0.0 0.0 copy-start
  0.0 11.2 %exchange.1 = (bf16[24,32,768]{2,1,0:T(8,128)(2,1)}, s32[16,8,128]{2,1,0:T(8,128)}) custom-call(bf16[24,32,1536]{2,1,0:T(8,128)(2,1)} %three.1, s32[1,2]{1,0:T(1,128)} %pairs.1), custom_call_target="tpu_custom_call" | custom-call | tf_op jit(solution)/shard_map/exchange/pallas_call | solution.py:88
  11.2 0.8 slice.32
  12.0 0.6 fusion.7
  16.4 0.0 copy-done.1
  16.5 0.6 fusion.6
  18.3 0.0 copy-done
  18.4 0.1 dynamic-slice_subtract_fusion
  18.4 0.0 copy-start.2
  18.4 2.2 %broadcast_select_fusion.1 = (bf16[24,32,768]{2,1,0:T(8,128)(2,1)S(1)}, bf16[24,32,768]{2,1,0:T(8,128)(2,1)S(1)}) fusion(bf16[24,32,768]{2,1,0:T(8,128)(2,1)} %get-tuple-element.8, pred[]{:T(512)S(6)} %eq.22, bf16[24,32,1536]{2,1,0:T(8,128)(2,1)} %three.1, s32[]{:T(128)S(6)} %select_n.65), kind=kLoop, calls=%fused_computation.8 | loop fusion | flops 1179648 | bytes 4718597 | tf_op jit(solution)/shard_map/jit(_where)/select_n | solution.py:418
  20.6 0.0 copy-done.2
  20.6 0.6 slice.37
  23.8 0.2 fusion.1
  24.0 0.7 slice_bitcast_fusion.3
  24.7 0.1 copy.8
  24.8 1.1 broadcast_select_fusion.b_msg
  25.9 1.3 stack.15
  27.2 3.0 %copy_dynamic-update-slice_fusion.1 = bf16[2,24,16,2,768]{4,1,0,2,3:T(8,128)(2,1)} fusion(bf16[1,24,16,2,768]{4,3,2,1,0:T(2,128)(2,1)} %stack.15), kind=kLoop, calls=%fused_computation.6 | loop fusion | bytes 2359296
  30.1 0.5 stack.16
  30.6 1.7 %copy_dynamic-update-slice_fusion = bf16[2,24,16,2,768]{4,1,0,2,3:T(8,128)(2,1)} fusion(bf16[2,24,16,2,768]{4,1,0,2,3:T(8,128)(2,1)} %copy_dynamic-update-slice_fusion.1, bf16[1,24,16,2,768]{4,3,2,1,0:T(2,128)(2,1)S(1)} %stack.16), kind=kLoop, calls=%fused_computation.5 | loop fusion | bytes 2359296 | tf_op jit(solution)/shard_map/stack | solution.py:418
  32.3 1.8 %fusion = bf16[2,24,16,768]{3,1,0,2:T(8,128)(2,1)S(1)} fusion(bf16[2,24,16,2,768]{4,1,0,2,3:T(8,128)(2,1)} %copy_dynamic-update-slice_fusion, pred[16]{0:T(512)(128)(4,1)S(1)} %get-tuple-element.14), kind=kLoop, calls=%fused_computation.3 | loop fusion | flops 589824 | bytes 3538960 | tf_op jit(solution)/shard_map/jit(_where)/select_n | solution.py:421
  34.2 0.1 dynamic_slice.24
  34.3 0.1 copy.12.eb
  34.4 116.7 %density.1 = f32[96,96]{1,0:T(8,128)S(1)} custom-call(bf16[16,48,768]{2,1,0:T(8,128)(2,1)S(1)} %bitcast.28, bf16[16,48,768]{2,1,0:T(8,128)(2,1)S(1)} %broadcast_select_fusion.b_msg, f32[192,1]{1,0:T(8,128)S(1)} %copy.12.eb, f32[1,768]{1,0:T(1,128)S(1)} %sub.15.ea), custom_call_target="tpu_custom_call" | custom-call | tf_op jit(solution)/shard_map/density/pallas_call | solution.py:357
  151.1 0.6 copy.17
  (4 shorter events, 0.0 us)
Async XLA Ops:
  0.0 16.4 %copy-start.1 = (f32[32]{0:T(128)S(1)}, f32[32]{0:T(128)}, u32[]{:S(2)}) copy-start(f32[32]{0:T(128)} %param.5) | copy-start | bytes 388
  0.0 18.3 %copy-start = (f32[1536]{0:T(1024)S(1)}, f32[1536]{0:T(1024)}, u32[]{:S(2)}) copy-start(f32[1536]{0:T(1024)} %param.6) | copy-start | bytes 18436
  18.4 2.2 %copy-start.2 = (s32[1,2]{1,0:T(1,128)S(1)}, s32[1,2]{1,0:T(1,128)}, u32[]{:S(2)}) copy-start(s32[1,2]{1,0:T(1,128)} %pairs.1) | copy-start | bytes 28

commit v2 on v0

v2 whole, which is shorter than its diff:
```python
import functools

import jax
import jax.numpy as jnp
from jax import lax
from jax.experimental import pallas as pl
from jax.experimental.pallas import tpu as pltpu
from jax.sharding import PartitionSpec as P

MESH = pl.DeviceIdType.MESH
F32 = jnp.float32
BF16 = jnp.bfloat16
I16 = jnp.int16
I32 = jnp.int32
NX, NY, NZ = 4, 4, 8
PLANE = NX * NY
PAIRS = 16
ROWS = 16
LANES = 128
STEPS = NZ // 2


def position():
    occ, aux = lax.axis_index("occ"), lax.axis_index("aux")
    core = lax.rem(aux, 2)
    x = lax.rem(lax.div(aux, 2), NX)
    z = lax.div(aux, 2 * NX) * 4 + lax.rem(occ, 4)
    return x, lax.div(occ, 4), z, core


def device(x, y, z, core):
    return (y * 4 + lax.rem(z, 4), (lax.div(z, 4) * NX + x) * 2 + core)


def remote(src, dst, send, recv, dev):
    return pltpu.make_async_remote_copy(
        src_ref=src, dst_ref=dst, send_sem=send, recv_sem=recv, device_id=dev, device_id_type=MESH
    )


def loop(first, last, body):
    def step(k, carry):
        body(k)
        return carry

    lax.fori_loop(first, last, step, 0)


def dot_rows(a, b):
    return lax.dot_general(a, b, (((0,), (0,)), ((), ())), preferred_element_type=F32)


def coded_rows(rows, columns):
    return rows * (columns // LANES) + ROWS


def encode(block, ref):
    rows, columns = block.shape
    groups = columns // LANES
    top = jnp.maximum(jnp.max(jnp.abs(block), axis=0, keepdims=True), 1e-30)
    level = jnp.ceil(jnp.log(top) * 64.0)
    codes = jnp.round(block * (32000.0 * jnp.exp(level * (-1.0 / 64.0)))).astype(I32).astype(I16)
    row = lax.broadcasted_iota(I32, (ROWS, LANES), 0)
    tail = jnp.zeros((ROWS, LANES), F32)
    for g in range(groups):
        ref[g * rows : (g + 1) * rows, :] = codes[:, g * LANES : (g + 1) * LANES]
        tail = jnp.where(row == g, level[:, g * LANES : (g + 1) * LANES], tail)
    ref[groups * rows : groups * rows + ROWS, :] = tail.astype(I32).astype(I16)


def decode(ref, rows):
    groups = (ref.shape[0] - ROWS) // rows
    tail = ref[groups * rows : groups * rows + ROWS, :].astype(I32).astype(F32)
    scale = jnp.exp(tail * (1.0 / 64.0)) * (1.0 / 32000.0)
    parts = [
        ref[g * rows : (g + 1) * rows, :].astype(I32).astype(F32) * scale[g : g + 1, :] for g in range(groups)
    ]
    return jnp.concatenate(parts, axis=1)


def density_kernel(
    sizes, three, occupied, virtual, pairs, out,
    mine, table, pick, rows_in, a_msg, b_msg, a_in, b_in, b_sib, coulomb, up_out, up_in, down_out, down_in, amp,
    high, low, left_high, left_low, dens, y_up0, y_up1, y_down0, y_down1, part, z_up, z_down,
    own_sem, half_send, half_recv, t_send, t_recv, a_send, a_recv, b_send, b_recv, s_send, s_recv,
    ring_send, ring_recv, x_send, x_recv, c_send, c_recv, y_send, y_recv, z_send, z_recv,
):
    half, width, slab, side = sizes
    x, y, z, core = position()
    occ, aux = lax.axis_index("occ"), lax.axis_index("aux")
    me = x * NY + y
    sibling = device(x, y, z, 1 - core)
    above, below = device(x, y, lax.rem(z + 1, NZ), core), device(x, y, lax.rem(z + NZ - 1, NZ), core)
    block_rows = rows_in.shape[1]
    orbitals = block_rows // ROWS

    def occ_peer(k):
        return (lax.rem(occ + k, PAIRS), aux)

    def peer(k):
        to = lax.rem(me + k, PLANE)
        return device(lax.div(to, NY), lax.rem(to, NY), z, core)

    rest = block_rows // 2

    def places(which):
        return rows_in.at[2 * which], rows_in.at[1, pl.ds(pl.multiple_of(which * rest, rest), rest)]

    def columns_of(which):
        return pl.ds(pl.multiple_of(which * half, LANES), half)

    here = places(core)
    own = [
        pltpu.make_async_copy(three.at[:block_rows, columns_of(core)], here[0], own_sem.at[0]),
        pltpu.make_async_copy(three.at[block_rows:, columns_of(core)], here[1], own_sem.at[1]),
    ]
    for copy in own:
        copy.start()
    mine[...] = jnp.zeros_like(mine)
    mine[0:1, 0:2] = pairs[...]

    barrier = pltpu.get_barrier_semaphore()
    loop(1, PAIRS, lambda k: pl.semaphore_signal(barrier, inc=1, device_id=occ_peer(k), device_id_type=MESH))
    loop(1, PLANE, lambda k: pl.semaphore_signal(barrier, inc=1, device_id=peer(k), device_id_type=MESH))
    for other in (sibling, above, below):
        pl.semaphore_signal(barrier, inc=1, device_id=other, device_id_type=MESH)
    pl.semaphore_wait(barrier, PAIRS - 1 + PLANE - 1 + 3)

    def row_out(k):
        return remote(mine, table.at[occ], t_send.at[k], t_recv.at[k], occ_peer(k))

    def row_in(k):
        came = lax.rem(occ + PAIRS - k, PAIRS)
        return remote(mine, table.at[came], t_send.at[k], t_recv.at[k], occ_peer(k))

    loop(1, PAIRS, lambda k: row_out(k).start())
    given = [
        remote(three.at[:block_rows, columns_of(1 - core)], here[0], half_send.at[0], half_recv.at[0], sibling),
        remote(three.at[block_rows:, columns_of(1 - core)], here[1], half_send.at[1], half_recv.at[1], sibling),
    ]
    for copy in given:
        copy.start()
    table[occ] = mine[...]

    lane = lax.broadcasted_iota(I32, (slab, 2 * half), 1)
    row = lax.broadcasted_iota(I32, (slab, 2 * half), 0)
    eb = []
    for q in range(2):
        first = lax.div(z, 4) * half + q * width + lax.rem(z, 4) * slab
        eb.append(jnp.sum(jnp.where(lane == row + first, virtual[...], 0.0), axis=1, keepdims=True))
    ea = [
        virtual[:, pl.ds(pl.multiple_of(core * half + q * width, LANES), width)] for q in range(2)
    ]

    loop(1, PAIRS, lambda k: row_in(k).wait_recv())
    orbital = lax.broadcasted_iota(I32, (1, occupied.shape[1]), 1)
    shift = jnp.zeros((1, 1), F32)
    for n in range(2):
        chosen = jnp.where(orbital == table[me, 0:1, n : n + 1], occupied[...], 0.0)
        shift = shift + jnp.sum(chosen, axis=1, keepdims=True)
    lane = lax.broadcasted_iota(I32, (ROWS, block_rows), 1)
    row = lax.broadcasted_iota(I32, (ROWS, block_rows), 0) * orbitals
    for n in range(2):
        for p in range(PAIRS):
            hit = lane == row + table[p, 0:1, n : n + 1]
            pick[n, p * ROWS : (p + 1) * ROWS, :] = jnp.where(hit, 1.0, 0.0).astype(BF16)
    for copy in own:
        copy.wait()
    for copy in given:
        copy.wait_recv()

    def plane_out(msg, into, send, recv, q, k):
        return remote(
            msg.at[q, lax.rem(me + k, PLANE)], into.at[q, me], send.at[q, k], recv.at[q, k], peer(k)
        )

    def plane_in(msg, into, send, recv, q, k):
        came = lax.rem(me + PLANE - k, PLANE)
        return remote(msg.at[q, came], into.at[q, came], send.at[q, k], recv.at[q, k], peer(k))

    a_refs, b_refs = (a_msg, a_in, a_send, a_recv), (b_msg, b_in, b_send, b_recv)

    def pick_rows(n, msg):
        for g in range(3):
            value = jnp.dot(pick[n], rows_in[g], preferred_element_type=F32).astype(BF16)
            for q in range(2):
                msg[q, :, g * ROWS : (g + 1) * ROWS, :] = value[:, q * width : (q + 1) * width].reshape(
                    PAIRS, ROWS, width
                )

    def send_plane(refs, q):
        loop(1, PLANE, lambda k: plane_out(*refs, q, k).start())
        refs[1][q, me] = refs[0][q, me]

    def to_sibling(q, k):
        came = lax.rem(me + PLANE - k, PLANE)
        return remote(b_in.at[q, came], b_sib.at[q, came], s_send.at[q, k], s_recv.at[q, k], sibling)

    def take_b(q):
        to_sibling(q, 0).start()

        def pass_on(k):
            plane_in(*b_refs, q, k).wait_recv()
            to_sibling(q, k).start()

        loop(1, PLANE, pass_on)

    def take_a(q):
        loop(1, PLANE, lambda k: plane_in(*a_refs, q, k).wait_recv())

    def take_sibling(q):
        loop(0, PLANE, lambda k: to_sibling(q, k).wait_recv())

    pick_rows(1, b_msg)
    send_plane(b_refs, 0)
    pick_rows(0, a_msg)
    send_plane(a_refs, 0)
    send_plane(a_refs, 1)
    send_plane(b_refs, 1)

    chunks = [(0, 0), (0, 1), (1, 0), (1, 1)]

    def multiply(n):
        q, r = chunks[n]
        right = a_in[r].reshape(-1, width)
        for source, which in ((b_in, core), (b_sib, 1 - core)):
            part_rows = pl.ds(pl.multiple_of(which * width, width), width)
            coulomb[n, part_rows, :] = dot_rows(source[q].reshape(-1, width), right)

    def block(n, w):
        return coulomb[n, pl.ds(pl.multiple_of(w * slab, slab), slab), :]

    mid = slab // 2
    short = coded_rows(mid, width)
    ways = ((0, up_out, up_in, above), (1, down_out, down_in, below))

    def hop(n, way, t):
        _, box, into, to = ways[way]
        slot = (n, t, slice(0, short)) if t == 0 else (n, t)
        return remote(box.at[slot], into.at[slot], ring_send.at[n, way, t], ring_recv.at[n, way, t], to)

    def ring(n, t):
        for way, box, into, _ in ways:
            w = lax.rem(z + 4 + t, NZ) if way else lax.rem(z + 4 - t, NZ)
            value = block(n, w)
            if t == 0:
                encode(value[mid:] if way else value[:mid], box.at[n, 0, :short])
            else:
                hop(n, way, t - 1).wait_recv()
                if t == 1:
                    came = decode(into.at[n, 0, :short], mid)
                    halves = [value[:mid], value[mid:]]
                    halves[way] = halves[way] + came
                    value = jnp.concatenate(halves, axis=0)
                else:
                    value = value + decode(into.at[n, t - 1], slab)
                encode(value, box.at[n, t])
            hop(n, way, t).start()

    x_next, x_prev, x_far = lax.rem(x + 1, NX), lax.rem(x + NX - 1, NX), lax.rem(x + 2, NX)
    lines = (x_next, x_prev, x_far)

    def line_out(n, i):
        q, r = chunks[n]
        ref = amp.at[core, r, x, q]
        return remote(ref, ref, x_send.at[n, i], x_recv.at[n, i], device(lines[i], y, z, core))

    def line_in(n, i):
        q, r = chunks[n]
        ref = amp.at[core, r, (x_prev, x_next, x_far)[i], q]
        return remote(ref, ref, x_send.at[n, i], x_recv.at[n, i], device(lines[i], y, z, core))

    def cross(n, i, which):
        q, r = chunks[n]
        ref = amp.at[which, r, (x_prev, x_next, x_far, x)[i], q]
        return remote(ref, ref, c_send.at[n, i], c_recv.at[n, i], sibling)

    def amplitude(n):
        q, r = chunks[n]
        hop(n, 0, STEPS - 1).wait_recv()
        hop(n, 1, STEPS - 1).wait_recv()
        total = block(n, z) + decode(up_in.at[n, STEPS - 1], slab) + decode(down_in.at[n, STEPS - 1], slab)
        encode(-total / (eb[q] + ea[r] - shift), amp.at[core, r, x, q])
        for i in range(3):
            line_out(n, i).start()
        cross(n, 3, core).start()

    def forward(n):
        for i in range(3):
            line_in(n, i).wait_recv()
            cross(n, i, core).start()

    turn = x * 2 + core
    turn_chunk, turn_shift = lax.div(turn, 4), lax.rem(width - side * lax.rem(turn, 4), width)

    def unpack(n):
        q, r = chunks[n]
        for i in range(4):
            cross(n, i, 1 - core).wait_recv()
        for h in range(2):
            for k in range(NX):
                value = decode(amp.at[h, r, k, q], slab)
                rows = slice((k * 2 + q) * slab, (k * 2 + q + 1) * slab)
                columns = slice(h * half + r * width, h * half + (r + 1) * width)
                top = value.astype(BF16)
                high[rows, columns] = top
                low[rows, columns] = (value - top.astype(F32)).astype(BF16)

    take_b(0)
    take_a(0)
    take_sibling(0)
    multiply(0)
    ring(0, 0)
    ring(0, 1)
    ring(0, 2)
    take_a(1)
    multiply(1)
    ring(1, 0)
    ring(0, 3)
    ring(1, 1)
    amplitude(0)
    take_b(1)
    take_sibling(1)
    multiply(2)
    ring(2, 0)
    ring(1, 2)
    multiply(3)
    ring(3, 0)
    ring(2, 1)
    ring(1, 3)
    ring(3, 1)
    forward(0)
    amplitude(1)
    ring(2, 2)
    ring(3, 2)
    ring(2, 3)
    unpack(0)
    forward(1)
    ring(3, 3)
    amplitude(2)
    unpack(1)
    amplitude(3)
    forward(2)
    unpack(2)
    forward(3)
    unpack(3)

    for h in range(2):
        for k in range(NX):
            for q in range(2):
                rows = slice((k * 2 + q) * slab, (k * 2 + q + 1) * slab)
                turned = pltpu.roll(decode(amp.at[h, turn_chunk, k, q], slab), turn_shift, 1)[:, 0:LANES]
                top = turned.astype(BF16)
                left_high[h, rows, :] = top
                left_low[h, rows, :] = (turned - top.astype(F32)).astype(BF16)
    wide = dens.shape[3]
    for h in range(2):
        for n in range(NY):
            columns = slice(n * wide, (n + 1) * wide)
            total = dot_rows(left_high[h], low[:, columns]) + dot_rows(left_low[h], high[:, columns])
            total = total + dot_rows(left_low[h], low[:, columns])
            dens[n, h] = (total + dot_rows(left_high[h], high[:, columns]))[0:side, :]

    y_next, y_prev, y_far = lax.rem(y + 1, NY), lax.rem(y + NY - 1, NY), lax.rem(y + 2, NY)
    north, south = device(x, y_next, z, core), device(x, y_prev, z, core)
    first = remote(dens.at[y_far, 0], y_up0, y_send.at[0], y_recv.at[0], north)
    second = remote(dens.at[y_far, 1], y_down0, y_send.at[1], y_recv.at[1], south)
    first.start()
    second.start()
    first.wait_recv()
    dens[y_next, 0] = dens[y_next, 0] + y_up0[...]
    third = remote(dens.at[y_next], y_up1, y_send.at[2], y_recv.at[2], north)
    third.start()
    second.wait_recv()
    dens[y_prev, 1] = dens[y_prev, 1] + y_down0[...]
    fourth = remote(dens.at[y_prev], y_down1, y_send.at[3], y_recv.at[3], south)
    fourth.start()
    third.wait_recv()
    fourth.wait_recv()
    for h in range(2):
        total = dens[y, h] + y_up1[h] + y_down1[h]
        for n in range(4):
            part[h * 4 + n] = total[:, n * side : (n + 1) * side]

    far_z = lax.rem(z + 4, NZ)
    cut = side // 2
    up_z = [remote(part.at[far_z, :cut], z_up.at[0, :cut], z_send.at[0], z_recv.at[0], above)]
    down_z = [remote(part.at[far_z, cut:], z_down.at[0, cut:], z_send.at[4], z_recv.at[4], below)]
    up_z[0].start()
    down_z[0].start()
    for t in range(1, STEPS):
        for way, sent, into, w, to in (
            (0, up_z, z_up, lax.rem(z + 4 - t, NZ), above),
            (1, down_z, z_down, lax.rem(z + 4 + t, NZ), below),
        ):
            sent[t - 1].wait_recv()
            if t > 1:
                part[w] = part[w] + into[t - 1]
            elif way:
                part[w, cut:] = part[w, cut:] + into[0, cut:]
            else:
                part[w, :cut] = part[w, :cut] + into[0, :cut]
            sent.append(remote(part.at[w], into.at[t], z_send.at[4 * way + t], z_recv.at[4 * way + t], to))
            sent[t].start()
    up_z[3].wait_recv()
    down_z[3].wait_recv()
    out[...] = part[z] + z_up[3] + z_down[3]

    for copy in given + [first, second, third, fourth] + up_z + down_z:
        copy.wait_send()
    loop(1, PAIRS, lambda k: row_out(k).wait_send())
    for q in range(2):
        loop(1, PLANE, lambda k, q=q: plane_out(*b_refs, q, k).wait_send())
        loop(1, PLANE, lambda k, q=q: plane_out(*a_refs, q, k).wait_send())
        loop(0, PLANE, lambda k, q=q: to_sibling(q, k).wait_send())
    for n in range(4):
        for way in range(2):
            for t in range(STEPS):
                hop(n, way, t).wait_send()
        for i in range(3):
            line_out(n, i).wait_send()
        for i in range(4):
            cross(n, i, core).wait_send()


def shards(three_index, occupied_energy, virtual_energy, pair_list):
    depth, orbitals, virtual = three_index.shape
    half = virtual // 2
    width = half // 2
    slab = width * 2 // NZ
    side = virtual // 16
    block_rows = ROWS * orbitals
    coded = coded_rows(slab, width)
    dma, vmem = pltpu.SemaphoreType.DMA, pltpu.VMEM
    inside = pl.BlockSpec(memory_space=vmem)
    message = (2, PLANE, 2 * depth, width)
    ring_box = (4, STEPS, coded, LANES)
    scratch = [
        vmem((8, LANES), I32),
        vmem((PAIRS, 8, LANES), I32),
        vmem((2, PAIRS * ROWS, block_rows), BF16),
        vmem((3, block_rows, half), BF16),
        *[vmem(message, BF16)] * 5,
        vmem((4, 2 * width, width), F32),
        *[vmem(ring_box, I16)] * 4,
        vmem((2, 2, NX, 2, coded, LANES), I16),
        *[vmem((NX * 2 * slab, virtual), BF16)] * 2,
        *[vmem((2, NX * 2 * slab, LANES), BF16)] * 2,
        vmem((NY, 2, side, virtual // NY), F32),
        *[vmem((side, virtual // NY), F32), vmem((2, side, virtual // NY), F32)] * 2,
        vmem((NZ, side, side), F32),
        *[vmem((STEPS, side, side), F32)] * 2,
        dma((2,)),
        *[dma((2,))] * 2,
        *[dma((PAIRS,))] * 2,
        *[dma((2, PLANE))] * 6,
        *[dma((4, 2, STEPS))] * 2,
        *[dma((4, 3))] * 2,
        *[dma((4, 4))] * 2,
        *[dma((4,))] * 2,
        *[dma((8,))] * 2,
    ]
    return pl.pallas_call(
        functools.partial(density_kernel, (half, width, slab, side)),
        out_shape=jax.ShapeDtypeStruct((side, side), F32),
        in_specs=[pl.BlockSpec(memory_space=pl.ANY), inside, inside, inside],
        out_specs=inside,
        scratch_shapes=scratch,
        compiler_params=pltpu.CompilerParams(
            collective_id=0, has_side_effects=True, vmem_limit_bytes=48 * 1024 * 1024
        ),
        name="density",
    )(
        three_index.reshape(depth * orbitals, virtual),
        occupied_energy.reshape(1, -1),
        virtual_energy.reshape(1, -1),
        pair_list,
    )


def solution(mesh):
    placed = (P(("occ", "aux"), None, None), P(), P(), P("occ", None))
    return jax.shard_map(shards, mesh=mesh, in_specs=placed, out_specs=P("aux", "occ"), check_vma=False)
```

time: 717 us -> 123 us (0.17)
  waiting for transfers between devices: 655 us -> 0 us
  Pallas kernels: 0 us -> 116 us
  between operations: 21.5 us -> 0.01 us
  matrix products: 17.9 us -> 0 us
  starting transfers between devices: 9.29 us -> 0 us
    reduce_scatter x3 -> x0, waiting for transfers between devices: 433 us -> none  [the longest x1 203 us: shards(): lax.psum_scatter(accumulated, 'occ', scatter_dimension=1, tiled=True)]
    psum x1 -> x0, waiting for transfers between devices: 171 us -> none  [broadcast(): return lax.psum(block, axis)]
    pallas_call x0 -> x1, Pallas kernels: none -> 116 us  [shards(): pl.pallas_call(functools.partial(density_kernel, (half, width, slab, side...]
    all_to_all x1 -> x0, waiting for transfers between devices: 50.5 us -> none  [shards(): lax.all_to_all(three_index, 'occ', split_axis=1, concat_axis=0, tiled=True)]
    dot_general x2 -> x0, matrix products: 17.9 us -> none  [the longest x1 11.5 us: shards(): lax.dot_general(amplitudes, amplitudes, (((0,), (0,)), ((), ())), precisi...]
    all_to_all x1 -> x0, starting transfers between devices: 9.13 us -> none  [shards(): lax.all_to_all(three_index, 'occ', split_axis=1, concat_axis=0, tiled=True)]
  transfers between devices with their start and end apart: 5 -> 0, of which waited for: 5 -> 0; matrix products, arithmetic and copies ran while one was open for 0% -> 0% of each run, Pallas kernels for 0% -> 0%
where the time goes in v2:
time: 123 us; the launch traced here: 120 us
  Pallas kernels  116 us (94%)
  local copies, waits for them, and re-layouts  4.3 us (3%)
    pallas_call x1, Pallas kernels, shards(): pl.pallas_call(functools.partial(density_kernel, (half, width, slab, side...  116 us
    unnamed x7, local copies, waits for them, and re-layouts  3.6 us

profile of v2, /device:TPU:8, one launch (start us, length us, event | category | flops | bytes accessed | tf_op | source)
XLA Modules:
  0.0 120.4 jit_solution(17421139713099813153)
XLA Ops:
  0.0 0.7 reshape.11.virtual
  0.7 0.0 copy-start
  0.7 1.7 %copy-done = bf16[24,32,1536]{2,1,0:T(8,128)(2,1)S(1)} copy-done((bf16[24,32,1536]{2,1,0:T(8,128)(2,1)S(1)}, bf16[24,32,1536]{2,1,0:T(8,128)(2,1)}, u32[]{:S(2)}) %copy-start) | copy-done | bytes 2359320
  2.4 0.0 copy-start.1
  2.4 0.7 copy-done.1
  3.0 0.0 copy-start.2
  3.0 0.7 copy-done.2
  3.7 116.1 %density.1 = f32[96,96]{1,0:T(8,128)S(1)} custom-call(bf16[768,1536]{1,0:T(8,128)(2,1)S(1)} %bitcast.2, f32[1,32]{1,0:T(1,128)S(1)} %bitcast.3, f32[1,1536]{1,0:T(1,128)S(1)} %reshape.11.virtual, s32[1,2]{1,0:T(1,128)S(1)} %copy-done.2), custom_call_target="tpu_custom_call" | custom-call | tf_op jit(solution)/shard_map/density/pallas_call | solution.py:463
  119.8 0.6 copy.6
Async XLA Ops:
  0.7 1.7 %copy-start = (bf16[24,32,1536]{2,1,0:T(8,128)(2,1)S(1)}, bf16[24,32,1536]{2,1,0:T(8,128)(2,1)}, u32[]{:S(2)}) copy-start(bf16[24,32,1536]{2,1,0:T(8,128)(2,1)} %param.4) | copy-start | bytes 7077892
  2.4 0.7 copy-start.1
  3.0 0.7 copy-start.2

commit v3 on v2

--- a/solution.py
+++ b/solution.py
@@ -79,11 +79,11 @@
 
 
 def density_kernel(
-    sizes, three, occupied, virtual, pairs, out,
-    mine, table, pick, rows_in, a_msg, b_msg, a_in, b_in, b_sib, coulomb, up_out, up_in, down_out, down_in, amp,
-    high, low, left_high, left_low, dens, y_up0, y_up1, y_down0, y_down1, part, z_up, z_down,
+    sizes, three, occupied_in, virtual_in, pairs_in, out,
+    occupied, virtual, pairs, mine, table, pick, rows_in, a_msg, b_msg, a_in, b_in, b_sib, coulomb, up_out, up_in, down_out, down_in, amp,
+    high, low, left_high, left_low, dens_a, y_up, y_down, part, z_up, z_down, dens_b, w_up, w_down, v_in,
     own_sem, half_send, half_recv, t_send, t_recv, a_send, a_recv, b_send, b_recv, s_send, s_recv,
-    ring_send, ring_recv, x_send, x_recv, c_send, c_recv, y_send, y_recv, z_send, z_recv,
+    ring_send, ring_recv, x_send, x_recv, c_send, c_recv, y_send, y_recv, z_send, z_recv, w_send, w_recv, v_send, v_recv,
 ):
     half, width, slab, side = sizes
     x, y, z, core = position()
@@ -114,16 +114,22 @@
         pltpu.make_async_copy(three.at[:block_rows, columns_of(core)], here[0], own_sem.at[0]),
         pltpu.make_async_copy(three.at[block_rows:, columns_of(core)], here[1], own_sem.at[1]),
     ]
-    for copy in own:
+    small = [
+        pltpu.make_async_copy(pairs_in, pairs, own_sem.at[2]),
+        pltpu.make_async_copy(virtual_in, virtual.at[0], own_sem.at[3]),
+        pltpu.make_async_copy(occupied_in, occupied.at[0], own_sem.at[4]),
+    ]
+    for copy in small + own:
         copy.start()
     mine[...] = jnp.zeros_like(mine)
-    mine[0:1, 0:2] = pairs[...]
 
     barrier = pltpu.get_barrier_semaphore()
     loop(1, PAIRS, lambda k: pl.semaphore_signal(barrier, inc=1, device_id=occ_peer(k), device_id_type=MESH))
     loop(1, PLANE, lambda k: pl.semaphore_signal(barrier, inc=1, device_id=peer(k), device_id_type=MESH))
     for other in (sibling, above, below):
         pl.semaphore_signal(barrier, inc=1, device_id=other, device_id_type=MESH)
+    small[0].wait()
+    mine[0:1, 0:2] = pairs[...]
     pl.semaphore_wait(barrier, PAIRS - 1 + PLANE - 1 + 3)
 
     def row_out(k):
@@ -142,6 +148,8 @@
         copy.start()
     table[occ] = mine[...]
 
+    small[1].wait()
+    small[2].wait()
     lane = lax.broadcasted_iota(I32, (slab, 2 * half), 1)
     row = lax.broadcasted_iota(I32, (slab, 2 * half), 0)
     eb = []
@@ -188,9 +196,10 @@
                     PAIRS, ROWS, width
                 )
 
-    def send_plane(refs, q):
-        loop(1, PLANE, lambda k: plane_out(*refs, q, k).start())
-        refs[1][q, me] = refs[0][q, me]
+    def send_plane(refs):
+        loop(1, PLANE, lambda k: plane_out(*refs, 0, k).start())
+        for q in range(2):
+            refs[1][q, me] = refs[0][q, me]
 
     def to_sibling(q, k):
         came = lax.rem(me + PLANE - k, PLANE)
@@ -202,21 +211,28 @@
         def pass_on(k):
             plane_in(*b_refs, q, k).wait_recv()
             to_sibling(q, k).start()
+            if q == 0:
+                plane_out(*b_refs, 0, k).wait_send()
+                plane_out(*a_refs, 1, k).start()
 
         loop(1, PLANE, pass_on)
 
     def take_a(q):
-        loop(1, PLANE, lambda k: plane_in(*a_refs, q, k).wait_recv())
+        def take(k):
+            plane_in(*a_refs, q, k).wait_recv()
+            if q == 0:
+                plane_out(*a_refs, 0, k).wait_send()
+                plane_out(*b_refs, 1, k).start()
+
+        loop(1, PLANE, take)
 
     def take_sibling(q):
         loop(0, PLANE, lambda k: to_sibling(q, k).wait_recv())
 
     pick_rows(1, b_msg)
-    send_plane(b_refs, 0)
+    send_plane(b_refs)
     pick_rows(0, a_msg)
-    send_plane(a_refs, 0)
-    send_plane(a_refs, 1)
-    send_plane(b_refs, 1)
+    send_plane(a_refs)
 
     chunks = [(0, 0), (0, 1), (1, 0), (1, 1)]
 
@@ -312,34 +328,34 @@
     multiply(0)
     ring(0, 0)
     ring(0, 1)
-    ring(0, 2)
     take_a(1)
     multiply(1)
     ring(1, 0)
+    ring(0, 2)
+    ring(1, 1)
     ring(0, 3)
-    ring(1, 1)
-    amplitude(0)
     take_b(1)
+    ring(1, 2)
     take_sibling(1)
     multiply(2)
     ring(2, 0)
-    ring(1, 2)
+    amplitude(0)
     multiply(3)
     ring(3, 0)
+    ring(1, 3)
     ring(2, 1)
-    ring(1, 3)
     ring(3, 1)
     forward(0)
     amplitude(1)
     ring(2, 2)
     ring(3, 2)
+    unpack(0)
     ring(2, 3)
-    unpack(0)
     forward(1)
     ring(3, 3)
     amplitude(2)
+    amplitude(3)
     unpack(1)
-    amplitude(3)
     forward(2)
     unpack(2)
     forward(3)
@@ -353,65 +369,104 @@
                 top = turned.astype(BF16)
                 left_high[h, rows, :] = top
                 left_low[h, rows, :] = (turned - top.astype(F32)).astype(BF16)
-    wide = dens.shape[3]
+    wide = dens_a.shape[3]
+    cut = side // 2
     for h in range(2):
         for n in range(NY):
             columns = slice(n * wide, (n + 1) * wide)
             total = dot_rows(left_high[h], low[:, columns]) + dot_rows(left_low[h], high[:, columns])
             total = total + dot_rows(left_low[h], low[:, columns])
-            dens[n, h] = (total + dot_rows(left_high[h], high[:, columns]))[0:side, :]
+            total = total + dot_rows(left_high[h], high[:, columns])
+            dens_a[n, h] = total[0:cut, :]
+            for i in range(4):
+                dens_b[h * 4 + i, n] = total[cut:side, i * side : (i + 1) * side]
 
     y_next, y_prev, y_far = lax.rem(y + 1, NY), lax.rem(y + NY - 1, NY), lax.rem(y + 2, NY)
     north, south = device(x, y_next, z, core), device(x, y_prev, z, core)
-    first = remote(dens.at[y_far, 0], y_up0, y_send.at[0], y_recv.at[0], north)
-    second = remote(dens.at[y_far, 1], y_down0, y_send.at[1], y_recv.at[1], south)
-    first.start()
-    second.start()
-    first.wait_recv()
-    dens[y_next, 0] = dens[y_next, 0] + y_up0[...]
-    third = remote(dens.at[y_next], y_up1, y_send.at[2], y_recv.at[2], north)
-    third.start()
-    second.wait_recv()
-    dens[y_prev, 1] = dens[y_prev, 1] + y_down0[...]
-    fourth = remote(dens.at[y_prev], y_down1, y_send.at[3], y_recv.at[3], south)
-    fourth.start()
-    third.wait_recv()
-    fourth.wait_recv()
-    for h in range(2):
-        total = dens[y, h] + y_up1[h] + y_down1[h]
-        for n in range(4):
-            part[h * 4 + n] = total[:, n * side : (n + 1) * side]
-
-    far_z = lax.rem(z + 4, NZ)
-    cut = side // 2
-    up_z = [remote(part.at[far_z, :cut], z_up.at[0, :cut], z_send.at[0], z_recv.at[0], above)]
-    down_z = [remote(part.at[far_z, cut:], z_down.at[0, cut:], z_send.at[4], z_recv.at[4], below)]
-    up_z[0].start()
-    down_z[0].start()
-    for t in range(1, STEPS):
-        for way, sent, into, w, to in (
-            (0, up_z, z_up, lax.rem(z + 4 - t, NZ), above),
-            (1, down_z, z_down, lax.rem(z + 4 + t, NZ), below),
-        ):
-            sent[t - 1].wait_recv()
-            if t > 1:
-                part[w] = part[w] + into[t - 1]
-            elif way:
-                part[w, cut:] = part[w, cut:] + into[0, cut:]
-            else:
-                part[w, :cut] = part[w, :cut] + into[0, :cut]
-            sent.append(remote(part.at[w], into.at[t], z_send.at[4 * way + t], z_recv.at[4 * way + t], to))
-            sent[t].start()
-    up_z[3].wait_recv()
-    down_z[3].wait_recv()
-    out[...] = part[z] + z_up[3] + z_down[3]
-
-    for copy in given + [first, second, third, fourth] + up_z + down_z:
+    up_y = [
+        remote(dens_a.at[w, h], y_up.at[i], y_send.at[i], y_recv.at[i], north)
+        for i, (w, h) in enumerate(((y_far, 0), (y_next, 1), (y_next, 0)))
+    ]
+    down_y = [
+        remote(dens_a.at[w, h], y_down.at[i], y_send.at[3 + i], y_recv.at[3 + i], south)
+        for i, (w, h) in enumerate(((y_far, 1), (y_prev, 0), (y_prev, 1)))
+    ]
+
+    def z_hop(rows, boxes, sems, way, t):
+        into, to = boxes[way], (above, below)[way]
+        w = lax.rem(z + 4 + t, NZ) if way else lax.rem(z + 4 - t, NZ)
+        part_of = rows.shape[1] // 2
+        some = (pl.ds(part_of, part_of) if way else pl.ds(0, part_of)) if t == 0 else slice(None)
+        return remote(
+            rows.at[w, some], into.at[t, some], sems[0].at[4 * way + t], sems[1].at[4 * way + t], to
+        )
+
+    def z_step(rows, boxes, sems, t):
+        part_of = rows.shape[1] // 2
+        for way in range(2):
+            w = lax.rem(z + 4 + t, NZ) if way else lax.rem(z + 4 - t, NZ)
+            if t > 0:
+                z_hop(rows, boxes, sems, way, t - 1).wait_recv()
+                some = (slice(part_of, None) if way else slice(0, part_of)) if t == 1 else slice(None)
+                rows[w, some] = rows[w, some] + boxes[way][t - 1, some]
+            z_hop(rows, boxes, sems, way, t).start()
+
+    def z_last(rows, boxes, sems):
+        z_hop(rows, boxes, sems, 0, STEPS - 1).wait_recv()
+        z_hop(rows, boxes, sems, 1, STEPS - 1).wait_recv()
+        return rows[z] + boxes[0][STEPS - 1] + boxes[1][STEPS - 1]
+
+    over_a = (part, (z_up, z_down), (z_send, z_recv))
+    over_b = (dens_b, (w_up, w_down), (w_send, w_recv))
+    for copy in (up_y[0], down_y[0], up_y[1], down_y[1]):
+        copy.start()
+    z_step(*over_b, 0)
+    up_y[0].wait_recv()
+    dens_a[y_next, 0] = dens_a[y_next, 0] + y_up[0]
+    up_y[2].start()
+    down_y[0].wait_recv()
+    dens_a[y_prev, 1] = dens_a[y_prev, 1] + y_down[0]
+    down_y[2].start()
+    z_step(*over_b, 1)
+    z_step(*over_b, 2)
+    for copy in up_y[1:] + down_y[1:]:
+        copy.wait_recv()
+    for h, came in ((0, y_up[2] + y_down[1]), (1, y_up[1] + y_down[2])):
+        total = dens_a[y, h] + came
+        for i in range(4):
+            part[h * 4 + i] = total[:, i * side : (i + 1) * side]
+    z_step(*over_a, 0)
+    z_step(*over_b, 3)
+    z_step(*over_a, 1)
+    summed = z_last(*over_b)
+    for n in range(NY):
+        v_in[0, n] = summed[n]
+
+    def column(i):
+        w = (y_next, y_prev, y_far)[i]
+        return remote(v_in.at[0, w], v_in.at[1 + i, 0], v_send.at[i], v_recv.at[i], device(x, w, z, core))
+
+    for i in range(3):
+        column(i).start()
+    z_step(*over_a, 2)
+    z_step(*over_a, 3)
+    for i in range(3):
+        column(i).wait_recv()
+    out[cut:, :] = v_in[0, y] + v_in[1, 0] + v_in[2, 0] + v_in[3, 0]
+    out[:cut, :] = z_last(*over_a)
+
+    for copy in given + up_y + down_y:
         copy.wait_send()
+    for over in (over_a, over_b):
+        for way in range(2):
+            for t in range(STEPS):
+                z_hop(*over, way, t).wait_send()
+    for i in range(3):
+        column(i).wait_send()
     loop(1, PAIRS, lambda k: row_out(k).wait_send())
+    loop(1, PLANE, lambda k: plane_out(*b_refs, 1, k).wait_send())
+    loop(1, PLANE, lambda k: plane_out(*a_refs, 1, k).wait_send())
     for q in range(2):
-        loop(1, PLANE, lambda k, q=q: plane_out(*b_refs, q, k).wait_send())
-        loop(1, PLANE, lambda k, q=q: plane_out(*a_refs, q, k).wait_send())
         loop(0, PLANE, lambda k, q=q: to_sibling(q, k).wait_send())
     for n in range(4):
         for way in range(2):
@@ -435,7 +490,11 @@
     inside = pl.BlockSpec(memory_space=vmem)
     message = (2, PLANE, 2 * depth, width)
     ring_box = (4, STEPS, coded, LANES)
+    cut = side // 2
     scratch = [
+        vmem((1, orbitals), F32),
+        vmem((1, virtual), F32),
+        vmem((1, 2), I32),
         vmem((8, LANES), I32),
         vmem((PAIRS, 8, LANES), I32),
         vmem((2, PAIRS * ROWS, block_rows), BF16),
@@ -446,34 +505,38 @@
         vmem((2, 2, NX, 2, coded, LANES), I16),
         *[vmem((NX * 2 * slab, virtual), BF16)] * 2,
         *[vmem((2, NX * 2 * slab, LANES), BF16)] * 2,
-        vmem((NY, 2, side, virtual // NY), F32),
-        *[vmem((side, virtual // NY), F32), vmem((2, side, virtual // NY), F32)] * 2,
-        vmem((NZ, side, side), F32),
-        *[vmem((STEPS, side, side), F32)] * 2,
-        dma((2,)),
+        vmem((NY, 2, cut, virtual // NY), F32),
+        *[vmem((3, cut, virtual // NY), F32)] * 2,
+        vmem((NZ, cut, side), F32),
+        *[vmem((STEPS, cut, side), F32)] * 2,
+        vmem((NZ, NY, cut, side), F32),
+        *[vmem((STEPS, NY, cut, side), F32)] * 2,
+        vmem((4, NY, cut, side), F32),
+        dma((5,)),
         *[dma((2,))] * 2,
         *[dma((PAIRS,))] * 2,
         *[dma((2, PLANE))] * 6,
         *[dma((4, 2, STEPS))] * 2,
         *[dma((4, 3))] * 2,
         *[dma((4, 4))] * 2,
-        *[dma((4,))] * 2,
-        *[dma((8,))] * 2,
+        *[dma((6,))] * 2,
+        *[dma((8,))] * 4,
+        *[dma((3,))] * 2,
     ]
     return pl.pallas_call(
         functools.partial(density_kernel, (half, width, slab, side)),
         out_shape=jax.ShapeDtypeStruct((side, side), F32),
-        in_specs=[pl.BlockSpec(memory_space=pl.ANY), inside, inside, inside],
+        in_specs=[pl.BlockSpec(memory_space=pltpu.HBM)] * 4,
         out_specs=inside,
         scratch_shapes=scratch,
         compiler_params=pltpu.CompilerParams(
-            collective_id=0, has_side_effects=True, vmem_limit_bytes=48 * 1024 * 1024
+            collective_id=0, has_side_effects=True, vmem_limit_bytes=62 * 1024 * 1024
         ),
         name="density",
     )(
         three_index.reshape(depth * orbitals, virtual),
-        occupied_energy.reshape(1, -1),
-        virtual_energy.reshape(1, -1),
+        occupied_energy,
+        virtual_energy,
         pair_list,
     )
 

time: 123 us -> 113 us (0.919); the launches traced: 120 us -> 113 us
  Pallas kernels: 116 us -> 111 us
  local copies, waits for them, and re-layouts: 4.3 us -> 1.42 us
    pallas_call x1, Pallas kernels: 116 us -> 111 us  [shards(): pl.pallas_call(functools.partial(density_kernel, (half, width, slab, side...]
    unnamed x7 -> x1, local copies, waits for them, and re-layouts: 3.6 us -> 1.42 us
where the time goes in v3:
time: 113 us
  Pallas kernels  111 us (98%)
  local copies, waits for them, and re-layouts  1.42 us (1%)
    pallas_call x1, Pallas kernels, shards(): pl.pallas_call(functools.partial(density_kernel, (half, width, slab, side...  111 us

profile of v3, /device:TPU:8, one launch (start us, length us, event | category | flops | bytes accessed | tf_op | source)
XLA Modules:
  0.0 112.8 jit_solution(7510118507724923924)
XLA Ops:
  0.0 111.3 %density.1 = f32[96,96]{1,0:T(8,128)} custom-call(bf16[768,1536]{1,0:T(8,128)(2,1)} %bitcast.1, f32[32]{0:T(128)} %occupied_in.1, f32[1536]{0:T(1024)} %virtual_in.1, s32[1,2]{1,0:T(1,128)} %pairs_in.1), custom_call_target="tpu_custom_call" | custom-call | tf_op jit(solution)/shard_map/density/pallas_call | solution.py:526
  111.3 1.4 %copy.6 = f32[96,96]{1,0:T(8,128)} copy(f32[96,96]{1,0:T(8,128)} %density.1) | data formatting | bytes 73728

commit v4 on v3

--- a/solution.py
+++ b/solution.py
@@ -44,6 +44,10 @@
         return carry
 
     lax.fori_loop(first, last, step, 0)
+
+
+def upper_rows(side):
+    return side * 7 // 12 // 8 * 8
 
 
 def dot_rows(a, b):
@@ -81,7 +85,7 @@
 def density_kernel(
     sizes, three, occupied_in, virtual_in, pairs_in, out,
     occupied, virtual, pairs, mine, table, pick, rows_in, a_msg, b_msg, a_in, b_in, b_sib, coulomb, up_out, up_in, down_out, down_in, amp,
-    high, low, left_high, left_low, dens_a, y_up, y_down, part, z_up, z_down, dens_b, w_up, w_down, v_in,
+    high, low, left, sums, dens_a, y_up, y_down, part, z_in, dens_b, w_up, w_down, v_in,
     own_sem, half_send, half_recv, t_send, t_recv, a_send, a_recv, b_send, b_recv, s_send, s_recv,
     ring_send, ring_recv, x_send, x_recv, c_send, c_recv, y_send, y_recv, z_send, z_recv, w_send, w_recv, v_send, v_recv,
 ):
@@ -97,9 +101,23 @@
     def occ_peer(k):
         return (lax.rem(occ + k, PAIRS), aux)
 
+    def z_peer(k):
+        return device(x, y, lax.rem(z + k, NZ), core)
+
+    def at_offset(k, sign):
+        step = lax.rem(k * 7, PLANE)
+        major, minor = lax.div(step, 4), lax.rem(step, 4)
+        dx = major * (1 - core) + minor * core
+        dy = minor * (1 - core) + major * core
+        return lax.rem(x + NX + sign * dx, NX), lax.rem(y + NY + sign * dy, NY)
+
+    def slot(k, sign):
+        to_x, to_y = at_offset(k, sign)
+        return to_x * NY + to_y
+
     def peer(k):
-        to = lax.rem(me + k, PLANE)
-        return device(lax.div(to, NY), lax.rem(to, NY), z, core)
+        to_x, to_y = at_offset(k, 1)
+        return device(to_x, to_y, z, core)
 
     rest = block_rows // 2
 
@@ -126,11 +144,12 @@
     barrier = pltpu.get_barrier_semaphore()
     loop(1, PAIRS, lambda k: pl.semaphore_signal(barrier, inc=1, device_id=occ_peer(k), device_id_type=MESH))
     loop(1, PLANE, lambda k: pl.semaphore_signal(barrier, inc=1, device_id=peer(k), device_id_type=MESH))
-    for other in (sibling, above, below):
+    loop(1, NZ, lambda k: pl.semaphore_signal(barrier, inc=1, device_id=z_peer(k), device_id_type=MESH))
+    for other in (sibling,):
         pl.semaphore_signal(barrier, inc=1, device_id=other, device_id_type=MESH)
     small[0].wait()
     mine[0:1, 0:2] = pairs[...]
-    pl.semaphore_wait(barrier, PAIRS - 1 + PLANE - 1 + 3)
+    pl.semaphore_wait(barrier, PAIRS - 1 + PLANE - 1 + NZ - 1 + 1)
 
     def row_out(k):
         return remote(mine, table.at[occ], t_send.at[k], t_recv.at[k], occ_peer(k))
@@ -179,11 +198,11 @@
 
     def plane_out(msg, into, send, recv, q, k):
         return remote(
-            msg.at[q, lax.rem(me + k, PLANE)], into.at[q, me], send.at[q, k], recv.at[q, k], peer(k)
+            msg.at[q, slot(k, 1)], into.at[q, me], send.at[q, k], recv.at[q, k], peer(k)
         )
 
     def plane_in(msg, into, send, recv, q, k):
-        came = lax.rem(me + PLANE - k, PLANE)
+        came = slot(k, -1)
         return remote(msg.at[q, came], into.at[q, came], send.at[q, k], recv.at[q, k], peer(k))
 
     a_refs, b_refs = (a_msg, a_in, a_send, a_recv), (b_msg, b_in, b_send, b_recv)
@@ -202,8 +221,8 @@
             refs[1][q, me] = refs[0][q, me]
 
     def to_sibling(q, k):
-        came = lax.rem(me + PLANE - k, PLANE)
-        return remote(b_in.at[q, came], b_sib.at[q, came], s_send.at[q, k], s_recv.at[q, k], sibling)
+        came = slot(k, -1)
+        return remote(b_in.at[q, came], b_sib.at[q, came], s_send.at[q, came], s_recv.at[q, came], sibling)
 
     def take_b(q):
         to_sibling(q, 0).start()
@@ -236,10 +255,11 @@
 
     chunks = [(0, 0), (0, 1), (1, 0), (1, 1)]
 
-    def multiply(n):
+    def multiply(n, sources=(0, 1)):
         q, r = chunks[n]
         right = a_in[r].reshape(-1, width)
-        for source, which in ((b_in, core), (b_sib, 1 - core)):
+        for i in sources:
+            source, which = ((b_in, core), (b_sib, 1 - core))[i]
             part_rows = pl.ds(pl.multiple_of(which * width, width), width)
             coulomb[n, part_rows, :] = dot_rows(source[q].reshape(-1, width), right)
 
@@ -316,11 +336,58 @@
         for h in range(2):
             for k in range(NX):
                 value = decode(amp.at[h, r, k, q], slab)
-                rows = slice((k * 2 + q) * slab, (k * 2 + q + 1) * slab)
+                rows = slice((q * NX + k) * slab, (q * NX + k + 1) * slab)
                 columns = slice(h * half + r * width, h * half + (r + 1) * width)
                 top = value.astype(BF16)
                 high[rows, columns] = top
                 low[rows, columns] = (value - top.astype(F32)).astype(BF16)
+
+    wide = dens_a.shape[3]
+    cut = upper_rows(side)
+
+    def turn_rows(q):
+        for h in range(2):
+            for k in range(NX):
+                rows = slice((q * NX + k) * slab, (q * NX + k + 1) * slab)
+                turned = pltpu.roll(decode(amp.at[h, turn_chunk, k, q], slab), turn_shift, 1)[:, 0:LANES]
+                top = turned.astype(BF16)
+                left[rows, 2 * h * LANES : (2 * h + 1) * LANES] = top
+                left[rows, (2 * h + 1) * LANES : (2 * h + 2) * LANES] = (turned - top.astype(F32)).astype(BF16)
+
+    y_next, y_prev, y_far = lax.rem(y + 1, NY), lax.rem(y + NY - 1, NY), lax.rem(y + 2, NY)
+    north, south = device(x, y_next, z, core), device(x, y_prev, z, core)
+    up_y = [
+        remote(dens_a.at[w, h], y_up.at[i], y_send.at[i], y_recv.at[i], north)
+        for i, (w, h) in enumerate(((y_far, 0), (y_next, 1), (y_next, 0)))
+    ]
+    down_y = [
+        remote(dens_a.at[w, h], y_down.at[i], y_send.at[3 + i], y_recv.at[3 + i], south)
+        for i, (w, h) in enumerate(((y_far, 1), (y_prev, 0), (y_prev, 1)))
+    ]
+
+    def product(q):
+        rows = slice(q * NX * slab, (q + 1) * NX * slab)
+        last = ((y_far, (up_y[0], down_y[0])), (y_next, up_y[1:2]), (y_prev, down_y[1:2]), (y, ()))
+        for n, ready in last if q else [(n, ()) for n in range(NY)]:
+            columns = pl.ds(pl.multiple_of(n * wide, LANES), wide)
+            by_high = dot_rows(left[rows, :], high[rows, columns])
+            by_low = dot_rows(left[rows, :], low[rows, columns])
+            for h in range(2):
+                first, second = 2 * h * LANES, (2 * h + 1) * LANES
+                total = by_low[second : second + side] + by_low[first : first + side]
+                total = total + by_high[second : second + side] + by_high[first : first + side]
+                if q == 0:
+                    sums[n, h] = total
+                    continue
+                total = total + sums[n, h]
+                dens_a[n, h] = total[0:cut, :]
+                for i in range(4):
+                    dens_b[h * 4 + i, n] = column_block(total[cut:side, :], i)
+            for copy in ready:
+                copy.start()
+
+    def column_block(rows, i):
+        return (pltpu.roll(rows, wide - i * side, 1) if i else rows)[:, 0:LANES]
 
     take_b(0)
     take_a(0)
@@ -335,13 +402,15 @@
     ring(1, 1)
     ring(0, 3)
     take_b(1)
+    multiply(2, (0,))
     ring(1, 2)
+    multiply(3, (0,))
     take_sibling(1)
-    multiply(2)
+    multiply(2, (1,))
     ring(2, 0)
+    multiply(3, (1,))
+    ring(3, 0)
     amplitude(0)
-    multiply(3)
-    ring(3, 0)
     ring(1, 3)
     ring(2, 1)
     ring(3, 1)
@@ -356,41 +425,14 @@
     amplitude(2)
     amplitude(3)
     unpack(1)
+    turn_rows(0)
     forward(2)
+    product(0)
+    forward(3)
     unpack(2)
-    forward(3)
     unpack(3)
-
-    for h in range(2):
-        for k in range(NX):
-            for q in range(2):
-                rows = slice((k * 2 + q) * slab, (k * 2 + q + 1) * slab)
-                turned = pltpu.roll(decode(amp.at[h, turn_chunk, k, q], slab), turn_shift, 1)[:, 0:LANES]
-                top = turned.astype(BF16)
-                left_high[h, rows, :] = top
-                left_low[h, rows, :] = (turned - top.astype(F32)).astype(BF16)
-    wide = dens_a.shape[3]
-    cut = side // 2
-    for h in range(2):
-        for n in range(NY):
-            columns = slice(n * wide, (n + 1) * wide)
-            total = dot_rows(left_high[h], low[:, columns]) + dot_rows(left_low[h], high[:, columns])
-            total = total + dot_rows(left_low[h], low[:, columns])
-            total = total + dot_rows(left_high[h], high[:, columns])
-            dens_a[n, h] = total[0:cut, :]
-            for i in range(4):
-                dens_b[h * 4 + i, n] = total[cut:side, i * side : (i + 1) * side]
-
-    y_next, y_prev, y_far = lax.rem(y + 1, NY), lax.rem(y + NY - 1, NY), lax.rem(y + 2, NY)
-    north, south = device(x, y_next, z, core), device(x, y_prev, z, core)
-    up_y = [
-        remote(dens_a.at[w, h], y_up.at[i], y_send.at[i], y_recv.at[i], north)
-        for i, (w, h) in enumerate(((y_far, 0), (y_next, 1), (y_next, 0)))
-    ]
-    down_y = [
-        remote(dens_a.at[w, h], y_down.at[i], y_send.at[3 + i], y_recv.at[3 + i], south)
-        for i, (w, h) in enumerate(((y_far, 1), (y_prev, 0), (y_prev, 1)))
-    ]
+    turn_rows(1)
+    product(1)
 
     def z_hop(rows, boxes, sems, way, t):
         into, to = boxes[way], (above, below)[way]
@@ -416,10 +458,10 @@
         z_hop(rows, boxes, sems, 1, STEPS - 1).wait_recv()
         return rows[z] + boxes[0][STEPS - 1] + boxes[1][STEPS - 1]
 
-    over_a = (part, (z_up, z_down), (z_send, z_recv))
     over_b = (dens_b, (w_up, w_down), (w_send, w_recv))
-    for copy in (up_y[0], down_y[0], up_y[1], down_y[1]):
-        copy.start()
+    def line(k):
+        return remote(part.at[lax.rem(z + k, NZ)], z_in.at[k], z_send.at[k], z_recv.at[k], z_peer(k))
+
     z_step(*over_b, 0)
     up_y[0].wait_recv()
     dens_a[y_next, 0] = dens_a[y_next, 0] + y_up[0]
@@ -434,10 +476,10 @@
     for h, came in ((0, y_up[2] + y_down[1]), (1, y_up[1] + y_down[2])):
         total = dens_a[y, h] + came
         for i in range(4):
-            part[h * 4 + i] = total[:, i * side : (i + 1) * side]
-    z_step(*over_a, 0)
+            part[h * 4 + i] = column_block(total, i)
+    for k in (4, 3, 5, 2, 6, 1, 7):
+        line(k).start()
     z_step(*over_b, 3)
-    z_step(*over_a, 1)
     summed = z_last(*over_b)
     for n in range(NY):
         v_in[0, n] = summed[n]
@@ -448,19 +490,22 @@
 
     for i in range(3):
         column(i).start()
-    z_step(*over_a, 2)
-    z_step(*over_a, 3)
+    total = part[z]
+    for k in (1, 7, 2, 6, 3, 5, 4):
+        line(k).wait_recv()
+        total = total + z_in[k]
+    out[:cut, :] = total[:, 0:side]
     for i in range(3):
         column(i).wait_recv()
-    out[cut:, :] = v_in[0, y] + v_in[1, 0] + v_in[2, 0] + v_in[3, 0]
-    out[:cut, :] = z_last(*over_a)
+    out[cut:, :] = (v_in[0, y] + v_in[1, 0] + v_in[2, 0] + v_in[3, 0])[:, 0:side]
 
     for copy in given + up_y + down_y:
         copy.wait_send()
-    for over in (over_a, over_b):
-        for way in range(2):
-            for t in range(STEPS):
-                z_hop(*over, way, t).wait_send()
+    for way in range(2):
+        for t in range(STEPS):
+            z_hop(*over_b, way, t).wait_send()
+    for k in range(1, NZ):
+        line(k).wait_send()
     for i in range(3):
         column(i).wait_send()
     loop(1, PAIRS, lambda k: row_out(k).wait_send())
@@ -490,7 +535,7 @@
     inside = pl.BlockSpec(memory_space=vmem)
     message = (2, PLANE, 2 * depth, width)
     ring_box = (4, STEPS, coded, LANES)
-    cut = side // 2
+    cut = upper_rows(side)
     scratch = [
         vmem((1, orbitals), F32),
         vmem((1, virtual), F32),
@@ -504,14 +549,15 @@
         *[vmem(ring_box, I16)] * 4,
         vmem((2, 2, NX, 2, coded, LANES), I16),
         *[vmem((NX * 2 * slab, virtual), BF16)] * 2,
-        *[vmem((2, NX * 2 * slab, LANES), BF16)] * 2,
+        vmem((NX * 2 * slab, 4 * LANES), BF16),
+        vmem((NY, 2, side, virtual // NY), F32),
         vmem((NY, 2, cut, virtual // NY), F32),
         *[vmem((3, cut, virtual // NY), F32)] * 2,
-        vmem((NZ, cut, side), F32),
-        *[vmem((STEPS, cut, side), F32)] * 2,
-        vmem((NZ, NY, cut, side), F32),
-        *[vmem((STEPS, NY, cut, side), F32)] * 2,
-        vmem((4, NY, cut, side), F32),
+        vmem((NZ, cut, LANES), F32),
+        vmem((NZ, cut, LANES), F32),
+        vmem((NZ, NY, side - cut, LANES), F32),
+        *[vmem((STEPS, NY, side - cut, LANES), F32)] * 2,
+        vmem((4, NY, side - cut, LANES), F32),
         dma((5,)),
         *[dma((2,))] * 2,
         *[dma((PAIRS,))] * 2,

time: 113 us -> 109 us (0.965)
  Pallas kernels: 111 us -> 107 us
    pallas_call x1, Pallas kernels: 111 us -> 107 us  [shards(): pl.pallas_call(functools.partial(density_kernel, (half, width, slab, side...]
where the time goes in v4:
time: 109 us; the launch traced here: 108 us
  Pallas kernels  107 us (98%)
  local copies, waits for them, and re-layouts  1.42 us (1%)
    pallas_call x1, Pallas kernels, shards(): pl.pallas_call(functools.partial(density_kernel, (half, width, slab, side...  107 us

profile of v4, /device:TPU:8, one launch (start us, length us, event | category | flops | bytes accessed | tf_op | source)
XLA Modules:
  0.0 108.1 jit_solution(4425460857853380812)
XLA Ops:
  0.0 106.7 %density.1 = f32[96,96]{1,0:T(8,128)} custom-call(bf16[768,1536]{1,0:T(8,128)(2,1)} %bitcast.1, f32[32]{0:T(128)} %occupied_in.1, f32[1536]{0:T(1024)} %virtual_in.1, s32[1,2]{1,0:T(1,128)} %pairs_in.1), custom_call_target="tpu_custom_call" | custom-call | tf_op jit(solution)/shard_map/density/pallas_call | solution.py:572
  106.7 1.4 %copy.6 = f32[96,96]{1,0:T(8,128)} copy(f32[96,96]{1,0:T(8,128)} %density.1) | data formatting | bytes 73728

commit v5 on v4

--- a/solution.py
+++ b/solution.py
@@ -427,8 +427,8 @@
     unpack(1)
     turn_rows(0)
     forward(2)
+    forward(3)
     product(0)
-    forward(3)
     unpack(2)
     unpack(3)
     turn_rows(1)

time: 109 us -> 108 us (level)
  no operation moved by 1% of the time
where the time goes in v5:
time: 108 us
  Pallas kernels  106 us (98%)
  local copies, waits for them, and re-layouts  1.42 us (1%)
    pallas_call x1, Pallas kernels, shards(): pl.pallas_call(functools.partial(density_kernel, (half, width, slab, side...  106 us

profile of v5, /device:TPU:8, one launch (start us, length us, event | category | flops | bytes accessed | tf_op | source)
XLA Modules:
  0.0 107.7 jit_solution(15043973489026832050)
XLA Ops:
  0.0 106.3 %density.1 = f32[96,96]{1,0:T(8,128)} custom-call(bf16[768,1536]{1,0:T(8,128)(2,1)} %bitcast.1, f32[32]{0:T(128)} %occupied_in.1, f32[1536]{0:T(1024)} %virtual_in.1, s32[1,2]{1,0:T(1,128)} %pairs_in.1), custom_call_target="tpu_custom_call" | custom-call | tf_op jit(solution)/shard_map/density/pallas_call | solution.py:572
  106.3 1.4 %copy.6 = f32[96,96]{1,0:T(8,128)} copy(f32[96,96]{1,0:T(8,128)} %density.1) | data formatting | bytes 73728
